TPU v7x, 256 devices: a whole 4x4x8 slice. The times are simulated.
256 devices in a mesh: leaf: 32 (over z, x), orb: 8 (over y, core).
Axes of the slice: x: 4, y: 4, z: 8, core: 2. Of those that a mesh axis runs over, the one named last changes fastest.
Arguments:
- orbitals: bfloat16 [160, 256, 16, 256], P('leaf', 'orb')
- potential: bfloat16 [160, 16, 256], P('leaf'), may hold values from 0.29882812 to 2
- counts: int32 [32], replicated, may hold values from 1 to 5, as said below
- neighbour_owner: int32 [160, 6], P('leaf'), may hold values from -1 to 31, as said below
- neighbour_slot: int32 [160, 6], P('leaf'), may hold values from 0 to 4, as said below
- pair_factor: bfloat16 [7, 256, 4, 256], replicated, may hold values from -0.0625 to 0.0625
- axis_factor: bfloat16 [7, 4, 16, 16], replicated, may hold values from -1.5 to 1.5
Outputs:
- rotated: bfloat16 [160, 256, 16, 256], P('leaf', 'orb')
Inputs may be any that keep to these rules, and one draw needn't show every extreme that they name: `counts`: counts of live boxes per subtree; they sum to 3 times the number of subtrees, and some subtree holds 5. `neighbour_owner`: for a live slot on subtree p the neighbour lies on subtree p - 1, p or p + 1, or is absent (-1); empty slots hold -1 everywhere. `neighbour_slot`: A neighbour points to a live slot; on the subtree below it is one of that subtree's last min(2, count) live slots, on the subtree above one of its first min(2, count) slots, and both ends of this range are used in every draw; absent neighbours hold 0.
All inputs are finite; a program needn't handle non-finite values.
Results may differ from a plain program's by a relative error of at most 0.0013.
The roundings to bfloat16 on the way count: a program that leaves them out, or rounds other values in their place, can miss the bound.
Values may be sent and summed in bfloat16 or wider, within the bound.
A program may use at most 128 MiB of HBM per device.

v0:
```python
import jax
import jax.numpy as jnp
from jax import lax
from jax.sharding import PartitionSpec as P


def extended_2(value, sides, width):
    for axis, dim in sides:
        size, length = (lax.axis_size(axis), value.shape[dim])
        up = [(i, (i + 1) % size) for i in range(size - 1)]
        down = [(j, i) for i, j in up]
        last = lax.slice_in_dim(value, length - width, length, axis=dim)
        leading = lax.slice_in_dim(value, 0, width, axis=dim)
        before = lax.ppermute(last, axis, up)
        after = lax.ppermute(leading, axis, down)
        value = jnp.concatenate([before, value, after], axis=dim)
    return value


def lookup(table, position):
    places = jnp.arange(table.shape[0], dtype=jnp.int32)
    return jnp.sum(jnp.where(places == position, table, 0))


def on_device(
    orbitals, potential, counts, neighbour_owner, neighbour_slot, pair_factor, axis_factor
):
    slots, orb_local, depth, paired = orbitals.shape
    terms = pair_factor.shape[2]
    product = (orbitals.astype(jnp.float32) * potential[:, None].astype(jnp.float32)).astype(
        jnp.bfloat16
    )
    position = lax.axis_index("leaf")
    count_here = lookup(counts, position)
    relative = neighbour_owner - position
    absent = neighbour_owner < 0
    zero_block = jnp.zeros((1, orb_local, depth, paired), jnp.bfloat16)
    extended = extended_2(product, (("leaf", 0),), slots)
    source_pool = jnp.concatenate([extended, zero_block], axis=0)
    index_table = jnp.where(
        absent,
        3 * slots,
        jnp.where(
            relative == 0,
            slots + neighbour_slot,
            jnp.where(relative < 0, neighbour_slot, 2 * slots + neighbour_slot),
        ),
    )
    total = jnp.zeros((slots * orb_local, depth, paired), jnp.float32)
    for direction in range(7):
        if direction < 6:
            sources = jnp.take(source_pool, index_table[:, direction], axis=0)
        else:
            sources = product
        flat = sources.reshape(slots * orb_local * depth, paired)
        inner = jnp.dot(
            flat,
            pair_factor[direction].reshape(paired, terms * paired),
            preferred_element_type=jnp.float32,
        )
        inner = inner.astype(jnp.bfloat16).reshape(slots * orb_local, depth, terms, paired)
        total = total + jnp.einsum(
            "bzrp,rzw->bwp", inner, axis_factor[direction], preferred_element_type=jnp.float32
        )
    live_mask = jnp.arange(slots, dtype=jnp.int32) < count_here
    total = total.reshape(slots, orb_local, depth, paired)
    propagated = jnp.where(live_mask[:, None, None, None], total, 0.0).astype(jnp.bfloat16)
    spread_out = lax.all_to_all(propagated, "orb", split_axis=2, concat_axis=1, tiled=True)
    partial_value = jnp.einsum(
        "sizp,sjzp->ij", spread_out, spread_out, preferred_element_type=jnp.float32
    )
    intersection = lax.psum(partial_value, ("leaf", "orb"))
    orb_total = intersection.shape[0]
    scale = jnp.trace(intersection) / orb_total
    identity = jnp.eye(orb_total, dtype=jnp.float32)
    rotation = ((1.5 * identity - 0.5 * intersection / scale) / jnp.sqrt(scale)).astype(
        jnp.bfloat16
    )
    turned = jnp.einsum(
        "sizp,ij->sjzp", spread_out, rotation, preferred_element_type=jnp.float32
    ).astype(jnp.bfloat16)
    return lax.all_to_all(turned, "orb", split_axis=1, concat_axis=2, tiled=True)


def solution(mesh):
    placed = (
        P("leaf", "orb", None, None),
        P("leaf", None, None),
        P(),
        P("leaf", None),
        P("leaf", None),
        P(),
        P(),
    )
    return jax.shard_map(
        on_device,
        mesh=mesh,
        in_specs=placed,
        out_specs=P("leaf", "orb", None, None),
        check_vma=False,
    )
```

profile of v0, /device:TPU:1, one launch (start us, length us, event | category | flops | bytes accessed | tf_op | source)
XLA Modules:
  0.0 503.9 jit_solution(11977119187600483710)
XLA Ops:
  6.5 0.8 convert_element_type.45
  7.4 1.6 multiply_convert_fusion
  9.0 1.3 collective-permute-start.1
  10.3 5.6 %collective-permute-start = (bf16[5,32,16,256]{3,2,1,0:T(8,128)(2,1)S(1)}, bf16[5,32,16,256]{3,2,1,0:T(8,128)(2,1)}, u32[]{:S(2)}, u32[]{:S(2)}) collective-permute-start(bf16[5,32,16,256]{3,2,1,0:T(8,128)(2,1)S(1)} %multiply_convert_fusion), channel_id=1, source_target_pairs={{0,8},{8,16},{16,24},{24,32},{32,40},{40,48},{48,56},{56,64},{64,7... | collective-permute-start | bytes 3932168 | tf_op jit(solution)/shard_map/ppermute | solution.py:14
  15.9 0.6 fusion.39
  16.5 0.3 slice_reduce_fusion.5
  16.9 3.3 fusion.43
  20.2 0.1 copy.61
  20.3 0.9 copy.65
  21.2 0.9 copy.64
  22.1 0.9 copy.63
  23.0 0.9 copy.62
  23.9 0.1 copy.67
  24.0 0.9 copy.66
  24.9 3.9 convolution_convert_fusion
  28.8 9.6 %reshape.69 = bf16[160,16,4,256]{3,2,1,0:T(4,128)(2,1)} reshape(bf16[2560,1024]{1,0:T(8,128)(2,1)} %convolution_convert_fusion) | data formatting | bytes 10485760 | tf_op jit(solution)/shard_map/reshape | solution.py:61
  38.4 0.6 iota_compare_fusion.1
  39.1 4.9 fusion
  44.0 3.5 maximum_maximum_fusion
  47.5 3.9 gather_fusion.5
  51.5 2.8 gather_fusion.4
  54.3 4.0 gather_fusion.3
  58.3 4.0 gather_fusion.2
  62.2 4.0 gather_fusion.1
  66.2 2.8 gather_fusion
  69.0 1.6 broadcast_select_fusion
  70.6 3.9 convolution_convert_fusion.1
  74.5 9.5 %reshape.67 = bf16[160,16,4,256]{3,2,1,0:T(4,128)(2,1)} reshape(bf16[2560,1024]{1,0:T(8,128)(2,1)} %convolution_convert_fusion.1) | data formatting | bytes 10485760 | tf_op jit(solution)/shard_map/reshape | solution.py:61
  84.0 4.9 fusion.2
  88.9 0.2 broadcast_select_fusion.4
  89.1 0.8 copy-done.7
  89.9 3.9 convolution_convert_fusion.5
  93.8 9.5 %reshape.59 = bf16[160,16,4,256]{3,2,1,0:T(4,128)(2,1)} reshape(bf16[2560,1024]{1,0:T(8,128)(2,1)} %convolution_convert_fusion.5) | data formatting | bytes 10485760 | tf_op jit(solution)/shard_map/reshape | solution.py:61
  103.3 4.9 fusion.10
  108.2 0.2 broadcast_select_fusion.3
  108.4 0.8 copy-done.6
  109.3 3.9 convolution_convert_fusion.4
  113.2 9.5 %reshape.61 = bf16[160,16,4,256]{3,2,1,0:T(4,128)(2,1)} reshape(bf16[2560,1024]{1,0:T(8,128)(2,1)} %convolution_convert_fusion.4) | data formatting | bytes 10485760 | tf_op jit(solution)/shard_map/reshape | solution.py:61
  122.7 4.9 fusion.8
  127.6 0.2 broadcast_select_fusion.2
  127.8 0.8 copy-done.5
  128.6 3.9 convolution_convert_fusion.3
  132.5 9.5 %reshape.63 = bf16[160,16,4,256]{3,2,1,0:T(4,128)(2,1)} reshape(bf16[2560,1024]{1,0:T(8,128)(2,1)} %convolution_convert_fusion.3) | data formatting | bytes 10485760 | tf_op jit(solution)/shard_map/reshape | solution.py:61
  142.0 4.9 fusion.6
  146.9 0.2 broadcast_select_fusion.1
  147.0 0.8 copy-done.4
  147.9 3.9 convolution_convert_fusion.2
  151.8 9.5 %reshape.65 = bf16[160,16,4,256]{3,2,1,0:T(4,128)(2,1)} reshape(bf16[2560,1024]{1,0:T(8,128)(2,1)} %convolution_convert_fusion.2) | data formatting | bytes 10485760 | tf_op jit(solution)/shard_map/reshape | solution.py:61
  161.3 4.9 fusion.4
  166.2 0.2 broadcast_select_fusion.5
  166.4 3.9 convolution_convert_fusion.6
  170.2 9.7 %reshape.57 = bf16[160,16,4,256]{3,2,1,0:T(4,128)(2,1)} reshape(bf16[2560,1024]{1,0:T(8,128)(2,1)} %convolution_convert_fusion.6) | data formatting | bytes 10485760 | tf_op jit(solution)/shard_map/reshape | solution.py:61
  179.9 7.6 %bitcast_add_fusion = bf16[160,256,16]{1,2,0:T(8,128)(2,1)S(1)} fusion(f32[160,256,16,1]{1,2,3,0:T(8,128)S(1)} %copy-done, f32[160,256,16,1]{1,2,3,0:T(8,128)} %fusion.2, f32[160,256,16,1]{1,2,3,0:T(8,128)} %fusion.4, f32[160,256,16,1]{1,2,3,0:T(8,128)} %fusion.6, f32[160,256,16,1]{1,2,3,0:T(8,128)} %fusion.8, f32[160,256,16,1]{1,2,3,0:T(8,128)} %fusion.10, ...), kind=kOutput, calls=%fused_computation.28 | convolution fusion | flops 88473600 | bytes 22298624 | tf_op jit(solution)/shard_map/bzrp,rzw->bwp/dot_general | solution.py:62
  187.5 0.5 fusion.14
  188.0 23.7 %all_to_all.36 = bf16[5,32,16,256]{3,1,0,2:T(8,128)(2,1)S(1)} all-to-all(bf16[5,32,16,256]{3,1,0,2:T(8,128)(2,1)S(1)} %fusion.14), channel_id=1, replica_groups=mesh['leaf'=32,'orb'=8] {'orb'}, dimensions={2} | all-to-all | bytes 2621440 | tf_op jit(solution)/shard_map/all_to_all | solution.py:68
  211.7 0.1 copy.40
  211.8 1.2 convolution_bitcast_fusion
  213.1 252.5 %all-reduce.2.cloned.1.call-done = f32[256,256]{1,0:T(8,128)} async-done(((f32[256,256]{1,0:T(8,128)}), f32[256,256]{1,0:T(8,128)}) %all-reduce.2.cloned.1.call-update) | async-done | bytes 262160 | tf_op jit(solution)/shard_map/psum | solution.py:72
  465.6 1.6 select_reduce_fusion
  467.9 1.5 fusion.17
  469.4 1.3 copy.42
  470.7 24.0 %all_to_all.37 = bf16[5,256,2,256]{3,2,0,1:T(2,128)(2,1)S(1)} all-to-all(bf16[5,256,2,256]{3,2,0,1:T(2,128)(2,1)S(1)} %copy.42), channel_id=1, replica_groups=mesh['leaf'=32,'orb'=8] {'orb'}, dimensions={1} | all-to-all | bytes 2621440 | tf_op jit(solution)/shard_map/all_to_all | solution.py:82
  494.7 1.0 copy.43
  495.7 1.4 all_to_all.33
  (40 shorter events, 0.2 us)
Async XLA Ops:
  6.5 9.4 %copy-start.12 = (s32[32]{0:T(128)S(1)}, s32[32]{0:T(128)}, u32[]{:S(2)}) copy-start(s32[32]{0:T(128)} %param.11) | copy-start | bytes 388
  6.5 10.0 %copy-start.10 = (s32[5,6]{1,0:T(8,128)S(1)}, s32[5,6]{1,0:T(8,128)}, u32[]{:S(2)}) copy-start(s32[5,6]{1,0:T(8,128)} %param.13) | copy-start | bytes 364
  6.5 10.0 %copy-start.11 = (s32[5,6]{1,0:T(8,128)S(1)}, s32[5,6]{1,0:T(8,128)}, u32[]{:S(2)}) copy-start(s32[5,6]{1,0:T(8,128)} %param.12) | copy-start | bytes 364
  6.5 459.1 %all-reduce.2.cloned.1.call-start = ((), (), s32[]{:S(2)}) async-start(), calls=%async_computation.2 | async-start | bytes 524288 | tf_op jit(solution)/shard_map/psum | solution.py:72
  9.0 35.0 %collective-permute-start.1 = (bf16[5,32,16,256]{3,2,1,0:T(8,128)(2,1)S(1)}, bf16[5,32,16,256]{3,2,1,0:T(8,128)(2,1)}, u32[]{:S(2)}, u32[]{:S(2)}) collective-permute-start(bf16[5,32,16,256]{3,2,1,0:T(8,128)(2,1)S(1)} %multiply_convert_fusion), channel_id=1, source_target_pairs={{8,0},{16,8},{24,16},{32,24},{40,32},{48,40},{56,48},{64,56},{72,6... | collective-permute-start | bytes 3932168 | tf_op jit(solution)/shard_map/ppermute | solution.py:15
  10.3 33.7 %collective-permute-start = (bf16[5,32,16,256]{3,2,1,0:T(8,128)(2,1)S(1)}, bf16[5,32,16,256]{3,2,1,0:T(8,128)(2,1)}, u32[]{:S(2)}, u32[]{:S(2)}) collective-permute-start(bf16[5,32,16,256]{3,2,1,0:T(8,128)(2,1)S(1)} %multiply_convert_fusion), channel_id=1, source_target_pairs={{0,8},{8,16},{16,24},{24,32},{32,40},{40,48},{48,56},{56,64},{64,7... | collective-permute-start | bytes 3932168 | tf_op jit(solution)/shard_map/ppermute | solution.py:14
  28.8 10.3 %copy-start.9 = (bf16[7,4,16,16]{3,2,1,0:T(8,128)(2,1)S(1)}, bf16[7,4,16,16]{3,2,1,0:T(8,128)(2,1)}, u32[]{:S(2)}) copy-start(bf16[7,4,16,16]{3,2,1,0:T(8,128)(2,1)} %param.15) | copy-start | bytes 43012
  69.0 1.6 copy-start.8
  84.0 4.9 copy-start.3
  88.9 1.0 copy-start.7
  103.3 4.9 copy-start.2
  108.2 1.0 copy-start.6
  122.7 4.9 copy-start.1
  127.6 1.0 copy-start.5
  146.9 1.0 copy-start.4
  170.2 9.7 %copy-start = (f32[160,256,16,1]{1,2,3,0:T(8,128)S(1)}, f32[160,256,16,1]{1,2,3,0:T(8,128)}, u32[]{:S(2)}) copy-start(f32[160,256,16,1]{1,2,3,0:T(8,128)} %fusion) | copy-start | bytes 7864324
Sparse Core Ops, SparseCore 0:
  213.2 252.3 all-reduce.1
where the time goes:
time: 506 us; the launch traced here: 504 us
  waiting for transfers between devices  253 us (50%)
  local copies, waits for them, and re-layouts  104 us (21%)
  matrix products  66.7 us (13%)
  blocking collectives  47.7 us (9%)
  between operations  14.4 us (3%)
  other arithmetic  11.9 us (2%)
  starting transfers between devices  6.93 us (1%)
    psum x1, waiting for transfers between devices, on_device(): intersection = lax.psum(partial_value, ('leaf', 'orb'))  253 us
    reshape x7, local copies, waits for them, and re-layouts, on_device(): inner.astype(jnp.bfloat16).reshape(slots * orb_local, depth, terms, paired)  66.8 us
    dot_general x7, matrix products, on_device(): jnp.einsum('bzrp,rzw->bwp', inner, axis_factor[direction], preferred_elem...  36.9 us
    dot_general x7, matrix products, on_device(): jnp.dot(flat, pair_factor[direction].reshape(paired, terms * paired), pre...  27.1 us
    all_to_all x1, blocking collectives, on_device(): lax.all_to_all(turned, 'orb', split_axis=1, concat_axis=2, tiled=True)  24 us
    all_to_all x1, blocking collectives, on_device(): lax.all_to_all(propagated, 'orb', split_axis=2, concat_axis=1, tiled=True)  23.7 us
    gather x6, local copies, waits for them, and re-layouts, on_device(): sources = jnp.take(source_pool, index_table[:, direction], axis=0)  21.4 us
  transfers between devices with their start and end apart: 3, of which 1 were waited for; matrix products, arithmetic and copies ran while one was open for 6% of the time, Pallas kernels for 0%

commit v1 on v0

v1 whole, which is shorter than its diff:
```python
import functools

import jax
import jax.numpy as jnp
from jax import lax
from jax.experimental import pallas as pl
from jax.experimental.pallas import tpu as pltpu
from jax.sharding import PartitionSpec as P

MESH = pl.DeviceIdType.MESH
F32 = jnp.float32
BF16 = jnp.bfloat16
CO = 8


def iota(shape, dim):
    return lax.broadcasted_iota(jnp.int32, shape, dim)


def kernel(
    dims,
    counts, owner, slot, potential, axis, orbitals, pair, out_hbm,
    table, live, pair_v, staged, spread, inner, source, send1, recv1, rows_v, S, part1, part2, full,
    send2, recv2, out_v, *rest,
):
    NL, NX, NO, SL, OL, D, PP, T = dims
    NC, NZ, G = OL // CO, NL // NX, NX * NO
    ZD = D // NO
    RO = CO * D
    N = OL * NO
    PR = N // G
    pools, orb_v = rest[:NC], rest[NC:2 * NC]
    (ld_sem, pair_sem, ex_send, ex_recv, a_send, a_recv, p1_send, p1_recv, p2_send, p2_recv, p3_send, p3_recv,
     b_send, b_recv, out_sem) = rest[2 * NC:]
    me_leaf, me = lax.axis_index("leaf"), lax.axis_index("orb")
    x, z = lax.rem(me_leaf, NX), me_leaf // NX
    m = x * NO + me

    loads = [
        pltpu.make_async_copy(orbitals.at[:, c * CO:(c + 1) * CO], orb_v[c], ld_sem.at[c])
        for c in range(NC)
    ]
    pair_load = pltpu.make_async_copy(pair, pair_v, pair_sem)
    loads[0].start()
    for load in loads[1:]:
        load.start()
    pair_load.start()

    def member(q):
        return (z * NX + q // NO, lax.rem(q, NO))

    barrier = pltpu.get_barrier_semaphore()
    up, down = lax.rem(me_leaf + 1, NL), lax.rem(me_leaf + NL - 1, NL)
    pl.semaphore_signal(barrier, inc=1, device_id=(up, me), device_id_type=MESH)
    pl.semaphore_signal(barrier, inc=1, device_id=(down, me), device_id_type=MESH)

    def greet(t, carry):
        pl.semaphore_signal(barrier, inc=1, device_id=member(lax.rem(m + t, G)), device_id_type=MESH)
        return carry

    lax.fori_loop(1, G, greet, 0)

    def greet_z(t, carry):
        pl.semaphore_signal(
            barrier, inc=1, device_id=(lax.rem(z + t, NZ) * NX + x, me), device_id_type=MESH)
        return carry

    lax.fori_loop(1, NZ, greet_z, 0)

    count = counts[me_leaf]
    count_low = counts[down]
    for g in range(SL):
        live[g] = (g < count).astype(jnp.int32)
        for d in range(6):
            own, at = owner[g, d], slot[g, d]
            low = SL + jnp.clip(at - count_low + 2, 0, 1)
            high = SL + 2 + jnp.clip(at, 0, 1)
            here = jnp.clip(at, 0, SL - 1)
            place = jnp.where(own == me_leaf, here, jnp.where(own < me_leaf, low, high))
            table[d * SL + g] = jnp.where(own < 0, SL + 4, place)
        table[6 * SL + g] = g

    def make_product(c):
        loads[c].wait()

        def block(g):
            value = orb_v[c][g].astype(F32) * potential[g].astype(F32)[None]
            return value.astype(BF16).reshape(RO, PP)

        for g in range(SL):
            pools[c][g] = block(g)
        pools[c][SL + 4] = jnp.zeros((RO, PP), BF16)
        for j in range(2):
            staged[c, j] = block(jnp.maximum(count - 2 + j, 0))

    def exchange(c):
        to_up = pltpu.make_async_remote_copy(
            src_ref=staged.at[c], dst_ref=pools[c].at[SL:SL + 2], send_sem=ex_send.at[c, 0],
            recv_sem=ex_recv.at[c, 0], device_id=(up, me), device_id_type=MESH)
        to_down = pltpu.make_async_remote_copy(
            src_ref=pools[c].at[0:2], dst_ref=pools[c].at[SL + 2:SL + 4], send_sem=ex_send.at[c, 1],
            recv_sem=ex_recv.at[c, 1], device_id=(down, me), device_id_type=MESH)
        return to_up, to_down

    exchanges = [exchange(c) for c in range(NC)]

    def start_exchange(c):
        for copy in exchanges[c]:
            copy.start()

    make_product(0)
    pl.semaphore_wait(barrier, G - 1 + NZ - 1 + 2)
    start_exchange(0)
    make_product(1)
    start_exchange(1)
    for c in range(2, NC):
        make_product(c)

    shift = CO.bit_length() - 1
    rise = (iota((RO, D), 0) >> shift == iota((RO, D), 1)).astype(BF16)
    TD = T * D
    lanes = T * RO
    wide_a, wide_b = iota((TD, lanes), 0), iota((TD, lanes), 1)
    widen = ((wide_a // D == wide_b // RO) & (lax.rem(wide_a, D) == lax.rem(wide_b, D))).astype(BF16)
    same = lax.rem(iota((RO, lanes), 0), CO) == lax.rem(iota((RO, lanes), 1), RO) // D

    for d in range(7):
        tall = lax.dot_general(rise, axis[d], (((1,), (1,)), ((), ())), preferred_element_type=F32).astype(BF16)
        full_d = jnp.dot(tall, widen, preferred_element_type=F32)
        spread[:, d * lanes:(d + 1) * lanes] = jnp.where(same, full_d, 0.0).astype(BF16)

    pair_load.wait()

    def pair_step(c, d):
        for g in range(SL):
            source[g * RO:(g + 1) * RO, :] = pools[c][table[d * SL + g]]
        for r in range(T):
            value = jnp.dot(source[...], pair_v[d, r], preferred_element_type=F32).astype(BF16)
            for g in range(SL):
                inner[c % 2, g, d, r] = value[g * RO:(g + 1) * RO]

    def self_step(c):
        for r in range(T):
            own_blocks = pools[c][0:SL].reshape(SL * RO, PP)
            value = jnp.dot(own_blocks, pair_v[6, r], preferred_element_type=F32).astype(BF16)
            for g in range(SL):
                inner[c % 2, g, 6, r] = value[g * RO:(g + 1) * RO]

    def to_peer(c, t):
        peer = lax.rem(me + t, NO)
        return pltpu.make_async_remote_copy(
            src_ref=send1.at[c, peer], dst_ref=recv1.at[me, c], send_sem=a_send.at[c, peer],
            recv_sem=a_recv.at[c, me], device_id=(me_leaf, peer), device_id_type=MESH)

    def from_peer(c, t):
        peer = lax.rem(me + NO - t, NO)
        return pltpu.make_async_remote_copy(
            src_ref=send1.at[c, peer], dst_ref=recv1.at[peer, c], send_sem=a_send.at[c, peer],
            recv_sem=a_recv.at[c, peer], device_id=(me_leaf, peer), device_id_type=MESH)

    def assemble(c):
        for t in range(1, NO):
            from_peer(c, t).wait_recv()
        for g in range(SL):
            block = recv1[:, c, g * ZD * CO:(g + 1) * ZD * CO, :].astype(F32).reshape(NO, ZD, CO, PP)
            for k in range(ZD):
                rows_v[g * ZD + k, c * NO * CO:(c + 1) * NO * CO, :] = (
                    block[:, k].reshape(NO * CO, PP).astype(BF16))

    self_step(0)
    self_step(1)
    for c in range(NC):
        for copy in exchanges[c]:
            copy.wait_recv()
        if c + 2 < NC:
            start_exchange(c + 2)
        if c >= 2:
            self_step(c)

        def over_d(d, carry, c=c):
            pair_step(c, d)
            return carry

        lax.fori_loop(0, 6, over_d, 0)

        def over_g(g, carry, c=c):
            weights = inner[c % 2, g].reshape(7 * T * RO, PP)
            total = jnp.dot(spread[...], weights, preferred_element_type=F32)
            total = jnp.where(live[g] > 0, total, 0.0).astype(BF16)
            rows = ZD * CO
            for j in range(NO):
                send1[c, j, pl.ds(pl.multiple_of(g * rows, rows), rows), :] = total[j * rows:(j + 1) * rows]
            return carry

        lax.fori_loop(0, SL, over_g, 0)
        for t in range(1, NO):
            to_peer(c, t).start()
        recv1[me, c] = send1[c, me]
        if c >= 1:
            assemble(c - 1)
    assemble(NC - 1)

    total = None
    for k in range(SL * ZD):
        block = rows_v[k]
        term = lax.dot_general(block, block, (((1,), (1,)), ((), ())), preferred_element_type=F32)
        total = term if total is None else total + term
    S[...] = total

    def p1(q_from, q_to, q_dev):
        return pltpu.make_async_remote_copy(
            src_ref=S.at[pl.ds(pl.multiple_of(q_to * PR, PR), PR)], dst_ref=part1.at[q_from],
            send_sem=p1_send.at[q_dev], recv_sem=p1_recv.at[q_from], device_id=member(q_dev), device_id_type=MESH)

    def p1_start(t, carry):
        q = lax.rem(m + t, G)
        p1(m, q, q).start()
        return carry

    lax.fori_loop(1, G, p1_start, 0)
    part1[m] = S[pl.ds(pl.multiple_of(m * PR, PR), PR)]

    def p1_wait(t, carry):
        q = lax.rem(m + G - t, G)
        p1(q, q, q).wait_recv()
        return carry

    lax.fori_loop(1, G, p1_wait, 0)
    part2[z] = jnp.sum(part1[...], axis=0)

    def p2(z_from, z_to):
        return pltpu.make_async_remote_copy(
            src_ref=part2.at[z_from], dst_ref=part2.at[z_from], send_sem=p2_send.at[z_to],
            recv_sem=p2_recv.at[z_from], device_id=(z_to * NX + x, me), device_id_type=MESH)

    for t in range(1, NZ):
        p2(z, lax.rem(z + t, NZ)).start()
    for t in range(1, NZ):
        other = lax.rem(z + NZ - t, NZ)
        p2(other, other).wait_recv()
    full[m] = jnp.sum(part2[...], axis=0)

    def p3(q_from, q_dev):
        return pltpu.make_async_remote_copy(
            src_ref=full.at[q_from], dst_ref=full.at[q_from], send_sem=p3_send.at[q_dev],
            recv_sem=p3_recv.at[q_from], device_id=member(q_dev), device_id_type=MESH)

    def p3_start(t, carry):
        q = lax.rem(m + t, G)
        p3(m, q).start()
        return carry

    lax.fori_loop(1, G, p3_start, 0)

    def p3_wait(t, carry):
        q = lax.rem(m + G - t, G)
        p3(q, q).wait_recv()
        return carry

    lax.fori_loop(1, G, p3_wait, 0)

    summed = full[...].reshape(N, N)
    diagonal = iota((N, N), 0) == iota((N, N), 1)
    trace = jnp.sum(jnp.sum(jnp.where(diagonal, summed, 0.0), axis=1, keepdims=True), axis=0, keepdims=True)
    scale = trace / N
    rotation = (jnp.where(diagonal, 1.5, 0.0) - 0.5 * summed / scale) / jnp.sqrt(scale)
    turn = jnp.transpose(rotation).astype(BF16)

    def back(g, a_from, a_to):
        return pltpu.make_async_remote_copy(
            src_ref=send2.at[a_to, g], dst_ref=recv2.at[a_from, g], send_sem=b_send.at[g, a_to],
            recv_sem=b_recv.at[g, a_from], device_id=(me_leaf, a_to), device_id_type=MESH)

    for g in range(SL):
        for k in range(ZD):
            value = jnp.dot(turn, rows_v[g * ZD + k], preferred_element_type=F32).reshape(NC, NO, CO, PP)
            for s in range(NO):
                send2[s, g, k * OL:(k + 1) * OL, :] = value[:, s].reshape(OL, PP).astype(BF16)
        for t in range(1, NO):
            back(g, me, lax.rem(me + t, NO)).start()
        recv2[me, g] = send2[me, g]

    row, column = iota((D * 16, D * 16), 0), iota((D * 16, D * 16), 1)
    swap = ((row // D == lax.rem(column, 16)) & (lax.rem(row, D) == column // 16)).astype(BF16)
    stores = []
    for g in range(SL):
        for t in range(1, NO):
            other = lax.rem(me + NO - t, NO)
            back(g, other, other).wait_recv()
        for h in range(OL // 16):
            block = recv2[:, g].reshape(NO, ZD, OL // 16, 16, PP)[:, :, h].reshape(D * 16, PP)
            value = jnp.dot(swap, block, preferred_element_type=F32).astype(BF16)
            out_v[g, h * 16:(h + 1) * 16] = value.reshape(16, D, PP)
        store = pltpu.make_async_copy(out_v.at[g], out_hbm.at[g], out_sem.at[g])
        store.start()
        stores.append(store)

    for pairs in exchanges:
        for copy in pairs:
            copy.wait_send()
    for c in range(NC):
        for t in range(1, NO):
            to_peer(c, t).wait_send()

    def drain(t, carry):
        q = lax.rem(m + t, G)
        p1(m, q, q).wait_send()
        p3(m, q).wait_send()
        return carry

    lax.fori_loop(1, G, drain, 0)
    for t in range(1, NZ):
        p2(z, lax.rem(z + t, NZ)).wait_send()
    for g in range(SL):
        for t in range(1, NO):
            back(g, me, lax.rem(me + t, NO)).wait_send()
    for store in stores:
        store.wait()


def on_device(dims, orbitals, potential, counts, owner, slot, pair, axis):
    NL, NX, NO, SL, OL, D, PP, T = dims
    NC, NZ, G = OL // CO, NL // NX, NX * NO
    ZD, RO, N = D // NO, CO * D, OL * NO
    PR = N // G
    vmem = pl.BlockSpec(memory_space=pltpu.VMEM)
    smem = pl.BlockSpec(memory_space=pltpu.SMEM)
    anywhere = pl.BlockSpec(memory_space=pl.ANY)
    dma = pltpu.SemaphoreType.DMA
    pair = pair.transpose(0, 2, 1, 3)
    return pl.pallas_call(
        functools.partial(kernel, dims),
        out_shape=jax.ShapeDtypeStruct(orbitals.shape, BF16),
        in_specs=[smem, smem, smem, vmem, vmem, anywhere, anywhere],
        out_specs=anywhere,
        scratch_shapes=[
            pltpu.SMEM((7 * SL,), jnp.int32),
            pltpu.SMEM((SL,), jnp.int32),
            pltpu.VMEM((7, T, PP, PP), BF16),
            pltpu.VMEM((NC, 2, RO, PP), BF16),
            pltpu.VMEM((RO, 7 * T * RO), BF16),
            pltpu.VMEM((2, SL, 7, T, RO, PP), BF16),
            pltpu.VMEM((SL * RO, PP), BF16),
            pltpu.VMEM((NC, NO, SL * ZD * CO, PP), BF16),
            pltpu.VMEM((NO, NC, SL * ZD * CO, PP), BF16),
            pltpu.VMEM((SL * ZD, N, PP), BF16),
            pltpu.VMEM((N, N), F32),
            pltpu.VMEM((G, PR, N), F32),
            pltpu.VMEM((NZ, PR, N), F32),
            pltpu.VMEM((G, PR, N), F32),
            pltpu.VMEM((NO, SL, ZD * OL, PP), BF16),
            pltpu.VMEM((NO, SL, ZD * OL, PP), BF16),
            pltpu.VMEM((SL, OL, D, PP), BF16),
            *[pltpu.VMEM((SL + 5, RO, PP), BF16) for _ in range(NC)],
            *[pltpu.VMEM((SL, CO, D, PP), BF16) for _ in range(NC)],
            dma((NC,)), dma(()), dma((NC, 2)), dma((NC, 2)),
            dma((NC, NO)), dma((NC, NO)),
            dma((G,)), dma((G,)), dma((NZ,)), dma((NZ,)), dma((G,)), dma((G,)),
            dma((SL, NO)), dma((SL, NO)), dma((SL,)),
        ],
        compiler_params=pltpu.CompilerParams(
            collective_id=0, has_side_effects=True, vmem_limit_bytes=56 * 2**20),
    )(counts, owner, slot, potential, axis.reshape(7, T * D, D), orbitals, pair)


def solution(mesh):
    leaf, orb = mesh.shape["leaf"], mesh.shape["orb"]
    along_x = 4 if leaf % 4 == 0 and leaf > 4 else 2

    def step(orbitals, potential, counts, owner, slot, pair, axis):
        slots, orbs, depth, paired = orbitals.shape
        dims = (leaf, along_x, orb, slots, orbs, depth, paired, pair.shape[2])
        return on_device(dims, orbitals, potential, counts, owner, slot, pair, axis)

    placed = (
        P("leaf", "orb", None, None),
        P("leaf", None, None),
        P(),
        P("leaf", None),
        P("leaf", None),
        P(),
        P(),
    )
    return jax.shard_map(
        step,
        mesh=mesh,
        in_specs=placed,
        out_specs=P("leaf", "orb", None, None),
        check_vma=False,
    )
```

time: 506 us -> 92.5 us (0.18)
  waiting for transfers between devices: 253 us -> 0 us
  local copies, waits for them, and re-layouts: 104 us -> 6.99 us
  Pallas kernels: 0 us -> 85.3 us
  matrix products: 66.7 us -> 0 us
  blocking collectives: 47.7 us -> 0 us
  between operations: 14.4 us -> 0.01 us
  other arithmetic: 11.9 us -> 0 us
  starting transfers between devices: 6.93 us -> 0 us
    psum x1 -> x0, waiting for transfers between devices: 253 us -> none  [on_device(): intersection = lax.psum(partial_value, ('leaf', 'orb'))]
    pallas_call x0 -> x1, Pallas kernels: none -> 85.3 us  [on_device(): pl.pallas_call(functools.partial(kernel, dims), out_shape=jax.ShapeDtypeS...]
    reshape x7 -> x0, local copies, waits for them, and re-layouts: 66.8 us -> none  [on_device(): inner.astype(jnp.bfloat16).reshape(slots * orb_local, depth, terms, paired)]
    dot_general x16 -> x0, matrix products: 66.7 us -> none  [the longest x7 36.9 us: on_device(): jnp.einsum('bzrp,rzw->bwp', inner, axis_factor[direction], preferred_elem...]
    all_to_all x2 -> x0, blocking collectives: 47.7 us -> none  [the longest x1 24 us: on_device(): lax.all_to_all(turned, 'orb', split_axis=1, concat_axis=2, tiled=True)]
    gather x6 -> x0, local copies, waits for them, and re-layouts: 21.4 us -> none  [on_device(): sources = jnp.take(source_pool, index_table[:, direction], axis=0)]
    ppermute x2 -> x0, starting transfers between devices: 6.93 us -> none  [the longest x1 5.64 us: extended_2(): before = lax.ppermute(last, axis, up)]
  transfers between devices with their start and end apart: 3 -> 0, of which waited for: 1 -> 0; matrix products, arithmetic and copies ran while one was open for 6% -> 0% of each run, Pallas kernels for 0% -> 0%
where the time goes in v1:
time: 92.5 us; the launch traced here: 92.3 us
  Pallas kernels  85.3 us (92%)
  local copies, waits for them, and re-layouts  6.99 us (8%)
    pallas_call x1, Pallas kernels, on_device(): pl.pallas_call(functools.partial(kernel, dims), out_shape=jax.ShapeDtypeS...  85.3 us
    unnamed x2, local copies, waits for them, and re-layouts  6.99 us

profile of v1, /device:TPU:1, one launch (start us, length us, event | category | flops | bytes accessed | tf_op | source)
XLA Modules:
  0.0 92.3 jit_solution(1622171228575849545)
XLA Ops:
  0.0 4.5 %copy.10 = bf16[7,256,4,256]{3,1,2,0:T(8,128)(2,1)} copy(bf16[7,256,4,256]{3,2,1,0:T(4,128)(2,1)} %param.12) | data formatting | bytes 7340032 | tf_op args[5]
  4.5 85.3 %shard_map.73 = bf16[5,32,16,256]{3,2,1,0:T(8,128)(2,1)} custom-call(s32[32]{0:T(128)} %counts.1, s32[5,6]{1,0:T(8,128)} %owner.1, s32[5,6]{1,0:T(8,128)} %slot.1, bf16[5,16,256]{2,1,0:T(8,128)(2,1)} %potential.1, bf16[7,64,16]{2,1,0:T(8,128)(2,1)} %bitcast.5, bf16[5,32,16,256]{3,2,1,0:T(8,128)(2,1)} %orbitals.1, bf16[7,4,256,256]{3,2,1,0:T(8,128)(2,1)} %bitcast.4), custom_call_target="tpu_custom_call" | custom-call | tf_op jit(solution)/shard_map/pallas_call | solution.py:331
  89.8 2.5 %copy.12 = bf16[5,32,16,256]{3,2,1,0:T(8,128)(2,1)} copy(bf16[5,32,16,256]{3,2,1,0:T(8,128)(2,1)} %shard_map.73) | data formatting | bytes 2621440

commit v2 on v1

--- a/solution.py
+++ b/solution.py
@@ -19,9 +19,9 @@
 
 def kernel(
     dims,
-    counts, owner, slot, potential, axis, orbitals, pair, out_hbm,
-    table, live, pair_v, staged, spread, inner, source, send1, recv1, rows_v, S, part1, part2, full,
-    send2, recv2, out_v, *rest,
+    counts, owner, slot, potential, axis, orbitals, pair, recv2,
+    table, live, raw_v, pair_v, staged, spread, inner, source, send1, recv1, rows_v, S, part1, part2, full,
+    send2, *rest,
 ):
     NL, NX, NO, SL, OL, D, PP, T = dims
     NC, NZ, G = OL // CO, NL // NX, NX * NO
@@ -40,7 +40,7 @@
         pltpu.make_async_copy(orbitals.at[:, c * CO:(c + 1) * CO], orb_v[c], ld_sem.at[c])
         for c in range(NC)
     ]
-    pair_load = pltpu.make_async_copy(pair, pair_v, pair_sem)
+    pair_load = pltpu.make_async_copy(pair, raw_v, pair_sem)
     loads[0].start()
     for load in loads[1:]:
         load.start()
@@ -111,9 +111,7 @@
     make_product(0)
     pl.semaphore_wait(barrier, G - 1 + NZ - 1 + 2)
     start_exchange(0)
-    make_product(1)
-    start_exchange(1)
-    for c in range(2, NC):
+    for c in range(1, NC):
         make_product(c)
 
     shift = CO.bit_length() - 1
@@ -130,6 +128,14 @@
         spread[:, d * lanes:(d + 1) * lanes] = jnp.where(same, full_d, 0.0).astype(BF16)
 
     pair_load.wait()
+    QB = PP // T
+    row, column = iota((PP, PP), 0), iota((PP, PP), 1)
+    sort = ((row // QB == lax.rem(column, T)) & (lax.rem(row, QB) == column // T)).astype(BF16)
+    for d in range(7):
+        for q in range(0, PP, QB):
+            block = jnp.dot(sort, raw_v[d, q:q + QB].reshape(PP, PP), preferred_element_type=F32).astype(BF16)
+            for r in range(T):
+                pair_v[d, r, q:q + QB] = block[r * QB:(r + 1) * QB]
 
     def pair_step(c, d):
         for g in range(SL):
@@ -146,27 +152,36 @@
             for g in range(SL):
                 inner[c % 2, g, 6, r] = value[g * RO:(g + 1) * RO]
 
-    def to_peer(c, t):
+    rows = ZD * CO
+
+    def between(c, g, here, there, peer):
+        at = pl.ds(0, SL * rows) if c < NC - 1 else pl.ds(g * rows, rows)
+        return pltpu.make_async_remote_copy(
+            src_ref=send1.at[c, there, at], dst_ref=recv1.at[here, c, at], send_sem=a_send.at[c + g, there],
+            recv_sem=a_recv.at[c + g, here], device_id=(me_leaf, peer), device_id_type=MESH)
+
+    def to_peer(c, t, g=0):
         peer = lax.rem(me + t, NO)
-        return pltpu.make_async_remote_copy(
-            src_ref=send1.at[c, peer], dst_ref=recv1.at[me, c], send_sem=a_send.at[c, peer],
-            recv_sem=a_recv.at[c, me], device_id=(me_leaf, peer), device_id_type=MESH)
-
-    def from_peer(c, t):
+        return between(c, g, me, peer, peer)
+
+    def from_peer(c, t, g=0):
         peer = lax.rem(me + NO - t, NO)
-        return pltpu.make_async_remote_copy(
-            src_ref=send1.at[c, peer], dst_ref=recv1.at[peer, c], send_sem=a_send.at[c, peer],
-            recv_sem=a_recv.at[c, peer], device_id=(me_leaf, peer), device_id_type=MESH)
+        return between(c, g, peer, peer, peer)
 
     def assemble(c):
-        for t in range(1, NO):
-            from_peer(c, t).wait_recv()
+        if c < NC - 1:
+            for t in range(1, NO):
+                from_peer(c, t).wait_recv()
         for g in range(SL):
-            block = recv1[:, c, g * ZD * CO:(g + 1) * ZD * CO, :].astype(F32).reshape(NO, ZD, CO, PP)
+            if c == NC - 1:
+                for t in range(1, NO):
+                    from_peer(c, t, g).wait_recv()
+            block = recv1[:, c, g * rows:(g + 1) * rows, :].astype(F32).reshape(NO, ZD, CO, PP)
             for k in range(ZD):
                 rows_v[g * ZD + k, c * NO * CO:(c + 1) * NO * CO, :] = (
                     block[:, k].reshape(NO * CO, PP).astype(BF16))
 
+    start_exchange(1)
     self_step(0)
     self_step(1)
     for c in range(NC):
@@ -177,24 +192,20 @@
         if c >= 2:
             self_step(c)
 
-        def over_d(d, carry, c=c):
+        for d in range(6):
             pair_step(c, d)
-            return carry
-
-        lax.fori_loop(0, 6, over_d, 0)
-
-        def over_g(g, carry, c=c):
+        for g in range(SL):
             weights = inner[c % 2, g].reshape(7 * T * RO, PP)
             total = jnp.dot(spread[...], weights, preferred_element_type=F32)
             total = jnp.where(live[g] > 0, total, 0.0).astype(BF16)
-            rows = ZD * CO
             for j in range(NO):
-                send1[c, j, pl.ds(pl.multiple_of(g * rows, rows), rows), :] = total[j * rows:(j + 1) * rows]
-            return carry
-
-        lax.fori_loop(0, SL, over_g, 0)
-        for t in range(1, NO):
-            to_peer(c, t).start()
+                send1[c, j, g * rows:(g + 1) * rows, :] = total[j * rows:(j + 1) * rows]
+            if c == NC - 1:
+                for t in range(1, NO):
+                    to_peer(c, t, g).start()
+        if c < NC - 1:
+            for t in range(1, NO):
+                to_peer(c, t).start()
         recv1[me, c] = send1[c, me]
         if c >= 1:
             assemble(c - 1)
@@ -271,6 +282,7 @@
             src_ref=send2.at[a_to, g], dst_ref=recv2.at[a_from, g], send_sem=b_send.at[g, a_to],
             recv_sem=b_recv.at[g, a_from], device_id=(me_leaf, a_to), device_id_type=MESH)
 
+    keeps = []
     for g in range(SL):
         for k in range(ZD):
             value = jnp.dot(turn, rows_v[g * ZD + k], preferred_element_type=F32).reshape(NC, NO, CO, PP)
@@ -278,29 +290,21 @@
                 send2[s, g, k * OL:(k + 1) * OL, :] = value[:, s].reshape(OL, PP).astype(BF16)
         for t in range(1, NO):
             back(g, me, lax.rem(me + t, NO)).start()
-        recv2[me, g] = send2[me, g]
-
-    row, column = iota((D * 16, D * 16), 0), iota((D * 16, D * 16), 1)
-    swap = ((row // D == lax.rem(column, 16)) & (lax.rem(row, D) == column // 16)).astype(BF16)
-    stores = []
+        keeps.append(pltpu.make_async_copy(send2.at[me, g], recv2.at[me, g], out_sem.at[g]))
+        keeps[-1].start()
+
     for g in range(SL):
         for t in range(1, NO):
             other = lax.rem(me + NO - t, NO)
             back(g, other, other).wait_recv()
-        for h in range(OL // 16):
-            block = recv2[:, g].reshape(NO, ZD, OL // 16, 16, PP)[:, :, h].reshape(D * 16, PP)
-            value = jnp.dot(swap, block, preferred_element_type=F32).astype(BF16)
-            out_v[g, h * 16:(h + 1) * 16] = value.reshape(16, D, PP)
-        store = pltpu.make_async_copy(out_v.at[g], out_hbm.at[g], out_sem.at[g])
-        store.start()
-        stores.append(store)
 
     for pairs in exchanges:
         for copy in pairs:
             copy.wait_send()
     for c in range(NC):
-        for t in range(1, NO):
-            to_peer(c, t).wait_send()
+        for g in range(SL if c == NC - 1 else 1):
+            for t in range(1, NO):
+                to_peer(c, t, g).wait_send()
 
     def drain(t, carry):
         q = lax.rem(m + t, G)
@@ -314,6 +318,25 @@
     for g in range(SL):
         for t in range(1, NO):
             back(g, me, lax.rem(me + t, NO)).wait_send()
+    for keep in keeps:
+        keep.wait()
+
+
+def settle(dims, blocks, out, held, placed, in_sem, out_sem):
+    NL, NX, NO, SL, OL, D, PP, T = dims
+    loads = [pltpu.make_async_copy(blocks.at[:, g], held.at[g], in_sem.at[g]) for g in range(SL)]
+    stores = [pltpu.make_async_copy(placed.at[g], out.at[g], out_sem.at[g]) for g in range(SL)]
+    for load in loads:
+        load.start()
+    row, column = iota((D * 16, D * 16), 0), iota((D * 16, D * 16), 1)
+    swap = ((row // D == lax.rem(column, 16)) & (lax.rem(row, D) == column // 16)).astype(BF16)
+    for g in range(SL):
+        loads[g].wait()
+        for h in range(OL // 16):
+            block = held[g].reshape(NO, D // NO, OL // 16, 16, PP)[:, :, h].reshape(D * 16, PP)
+            value = jnp.dot(swap, block, preferred_element_type=F32).astype(BF16)
+            placed[g, h * 16:(h + 1) * 16] = value.reshape(16, D, PP)
+        stores[g].start()
     for store in stores:
         store.wait()
 
@@ -327,15 +350,15 @@
     smem = pl.BlockSpec(memory_space=pltpu.SMEM)
     anywhere = pl.BlockSpec(memory_space=pl.ANY)
     dma = pltpu.SemaphoreType.DMA
-    pair = pair.transpose(0, 2, 1, 3)
-    return pl.pallas_call(
+    blocks = pl.pallas_call(
         functools.partial(kernel, dims),
-        out_shape=jax.ShapeDtypeStruct(orbitals.shape, BF16),
+        out_shape=jax.ShapeDtypeStruct((NO, SL, ZD * OL, PP), BF16),
         in_specs=[smem, smem, smem, vmem, vmem, anywhere, anywhere],
         out_specs=anywhere,
         scratch_shapes=[
             pltpu.SMEM((7 * SL,), jnp.int32),
             pltpu.SMEM((SL,), jnp.int32),
+            pltpu.VMEM((7, PP, T, PP), BF16),
             pltpu.VMEM((7, T, PP, PP), BF16),
             pltpu.VMEM((NC, 2, RO, PP), BF16),
             pltpu.VMEM((RO, 7 * T * RO), BF16),
@@ -349,18 +372,27 @@
             pltpu.VMEM((NZ, PR, N), F32),
             pltpu.VMEM((G, PR, N), F32),
             pltpu.VMEM((NO, SL, ZD * OL, PP), BF16),
-            pltpu.VMEM((NO, SL, ZD * OL, PP), BF16),
-            pltpu.VMEM((SL, OL, D, PP), BF16),
             *[pltpu.VMEM((SL + 5, RO, PP), BF16) for _ in range(NC)],
             *[pltpu.VMEM((SL, CO, D, PP), BF16) for _ in range(NC)],
             dma((NC,)), dma(()), dma((NC, 2)), dma((NC, 2)),
-            dma((NC, NO)), dma((NC, NO)),
+            dma((NC - 1 + SL, NO)), dma((NC - 1 + SL, NO)),
             dma((G,)), dma((G,)), dma((NZ,)), dma((NZ,)), dma((G,)), dma((G,)),
             dma((SL, NO)), dma((SL, NO)), dma((SL,)),
         ],
         compiler_params=pltpu.CompilerParams(
             collective_id=0, has_side_effects=True, vmem_limit_bytes=56 * 2**20),
     )(counts, owner, slot, potential, axis.reshape(7, T * D, D), orbitals, pair)
+    return pl.pallas_call(
+        functools.partial(settle, dims),
+        out_shape=jax.ShapeDtypeStruct(orbitals.shape, BF16),
+        in_specs=[anywhere],
+        out_specs=anywhere,
+        scratch_shapes=[
+            pltpu.VMEM((SL, NO, ZD * OL, PP), BF16),
+            pltpu.VMEM((SL, OL, D, PP), BF16),
+            dma((SL,)), dma((SL,)),
+        ],
+    )(blocks)
 
 
 def solution(mesh):

time: 92.5 us -> 83.9 us (0.907)
  local copies, waits for them, and re-layouts: 6.99 us -> 0 us
  Pallas kernels: 85.3 us -> 83.6 us
    unnamed x2 -> x0, local copies, waits for them, and re-layouts: 6.99 us -> none
    pallas_call x1, Pallas kernels: 85.3 us -> 80.7 us  [on_device(): pl.pallas_call(functools.partial(kernel, dims), out_shape=jax.ShapeDtypeS...]
    pallas_call x0 -> x1, Pallas kernels: none -> 2.91 us  [on_device(): pl.pallas_call(functools.partial(settle, dims), out_shape=jax.ShapeDtypeS...]
where the time goes in v2:
time: 83.9 us; the launch traced here: 83.8 us
  Pallas kernels  83.6 us (100%)
    pallas_call x1, Pallas kernels, on_device(): pl.pallas_call(functools.partial(kernel, dims), out_shape=jax.ShapeDtypeS...  80.7 us
    pallas_call x1, Pallas kernels, on_device(): pl.pallas_call(functools.partial(settle, dims), out_shape=jax.ShapeDtypeS...  2.91 us

profile of v2, /device:TPU:1, one launch (start us, length us, event | category | flops | bytes accessed | tf_op | source)
XLA Modules:
  0.0 83.8 jit_solution(13080247565661862087)
XLA Ops:
  0.0 80.7 %shard_map.73.blocks = bf16[8,5,64,256]{3,2,1,0:T(8,128)(2,1)} custom-call(s32[32]{0:T(128)} %counts.1, s32[5,6]{1,0:T(8,128)} %owner.1, s32[5,6]{1,0:T(8,128)} %slot.1, bf16[5,16,256]{2,1,0:T(8,128)(2,1)} %potential.1, bf16[7,64,16]{2,1,0:T(8,128)(2,1)} %bitcast.1, bf16[5,32,16,256]{3,2,1,0:T(8,128)(2,1)} %orbitals.1, bf16[7,256,4,256]{3,2,1,0:T(4,128)(2,1)} %pair.1), custom_call_target="tpu_custom_call" | custom-call | tf_op jit(solution)/shard_map/pallas_call | solution.py:353
  80.7 2.9 %shard_map.74 = bf16[5,32,16,256]{3,2,1,0:T(8,128)(2,1)} custom-call(bf16[8,5,64,256]{3,2,1,0:T(8,128)(2,1)} %shard_map.73.blocks), custom_call_target="tpu_custom_call" | custom-call | tf_op jit(solution)/shard_map/pallas_call | solution.py:385

commit v3 on v2

--- a/solution.py
+++ b/solution.py
@@ -17,10 +17,21 @@
     return lax.broadcasted_iota(jnp.int32, shape, dim)
 
 
+def split(value, size):
+    return value >> (size.bit_length() - 1), value & (size - 1)
+
+
+def reorder(outer, inner):
+    size = outer * inner
+    high, low = split(iota((size, size), 0), outer)
+    other_high, other_low = split(iota((size, size), 1), inner)
+    return ((high == other_low) & (low == other_high)).astype(BF16)
+
+
 def kernel(
     dims,
-    counts, owner, slot, potential, axis, orbitals, pair, recv2,
-    table, live, raw_v, pair_v, staged, spread, inner, source, send1, recv1, rows_v, S, part1, part2, full,
+    counts_in, owner_in, slot_in, potential_in, axis_in, orbitals, pair, recv2,
+    counts, owner, slot, potential, axis, table, live, raw_v, pair_v, staged, spread, inner, source, send1, recv1, rows_v, S, part1, part2, full,
     send2, *rest,
 ):
     NL, NX, NO, SL, OL, D, PP, T = dims
@@ -31,7 +42,7 @@
     PR = N // G
     pools, orb_v = rest[:NC], rest[NC:2 * NC]
     (ld_sem, pair_sem, ex_send, ex_recv, a_send, a_recv, p1_send, p1_recv, p2_send, p2_recv, p3_send, p3_recv,
-     b_send, b_recv, out_sem) = rest[2 * NC:]
+     b_send, b_recv, out_sem, small_sem, known) = rest[2 * NC:]
     me_leaf, me = lax.axis_index("leaf"), lax.axis_index("orb")
     x, z = lax.rem(me_leaf, NX), me_leaf // NX
     m = x * NO + me
@@ -41,10 +52,14 @@
         for c in range(NC)
     ]
     pair_load = pltpu.make_async_copy(pair, raw_v, pair_sem)
+    small = [
+        pltpu.make_async_copy(*ends, small_sem.at[i])
+        for i, ends in enumerate(
+            ((counts_in, counts), (potential_in, potential), (owner_in, owner), (slot_in, slot), (axis_in, axis)))
+    ]
     loads[0].start()
-    for load in loads[1:]:
+    for load in small:
         load.start()
-    pair_load.start()
 
     def member(q):
         return (z * NX + q // NO, lax.rem(q, NO))
@@ -53,21 +68,69 @@
     up, down = lax.rem(me_leaf + 1, NL), lax.rem(me_leaf + NL - 1, NL)
     pl.semaphore_signal(barrier, inc=1, device_id=(up, me), device_id_type=MESH)
     pl.semaphore_signal(barrier, inc=1, device_id=(down, me), device_id_type=MESH)
-
-    def greet(t, carry):
-        pl.semaphore_signal(barrier, inc=1, device_id=member(lax.rem(m + t, G)), device_id_type=MESH)
-        return carry
-
-    lax.fori_loop(1, G, greet, 0)
-
-    def greet_z(t, carry):
-        pl.semaphore_signal(
-            barrier, inc=1, device_id=(lax.rem(z + t, NZ) * NX + x, me), device_id_type=MESH)
-        return carry
-
-    lax.fori_loop(1, NZ, greet_z, 0)
-
+    for t in range(1, NO):
+        pl.semaphore_signal(barrier, inc=1, device_id=(me_leaf, lax.rem(me + t, NO)), device_id_type=MESH)
+
+    reaches = [1 << i for i in range(max(NL // 4, 1).bit_length())]
+
+    def tell(i):
+        d = reaches[i]
+        for to in (lax.rem(me_leaf + d, NL), lax.rem(me_leaf + NL - d, NL)):
+            pl.semaphore_signal(known.at[i], inc=1, device_id=(to, me), device_id_type=MESH)
+
+    def hear(i):
+        pl.semaphore_wait(known.at[i], 2)
+
+    def tell_orbs():
+        for t in range(1, NO):
+            pl.semaphore_signal(
+                known.at[len(reaches)], inc=1, device_id=(me_leaf, lax.rem(me + t, NO)), device_id_type=MESH)
+
+    for load in loads[1:]:
+        load.start()
+    pair_load.start()
+
+    small[0].wait()
+    small[1].wait()
     count = counts[me_leaf]
+
+    def make_product(c):
+        loads[c].wait()
+
+        def block(g):
+            value = orb_v[c][g].astype(F32) * potential[g].astype(F32)[None]
+            return value.astype(BF16).reshape(RO, PP)
+
+        for g in range(SL):
+            pools[c][g] = block(g)
+        pools[c][SL + 4] = jnp.zeros((RO, PP), BF16)
+        for j in range(2):
+            staged[c, j] = block(jnp.maximum(count - 2 + j, 0))
+
+    def exchange(c):
+        to_up = pltpu.make_async_remote_copy(
+            src_ref=staged.at[c], dst_ref=pools[c].at[SL:SL + 2], send_sem=ex_send.at[c, 0],
+            recv_sem=ex_recv.at[c, 0], device_id=(up, me), device_id_type=MESH)
+        to_down = pltpu.make_async_remote_copy(
+            src_ref=pools[c].at[0:2], dst_ref=pools[c].at[SL + 2:SL + 4], send_sem=ex_send.at[c, 1],
+            recv_sem=ex_recv.at[c, 1], device_id=(down, me), device_id_type=MESH)
+        return to_up, to_down
+
+    exchanges = [exchange(c) for c in range(NC)]
+
+    def start_exchange(c):
+        for copy in exchanges[c]:
+            copy.start()
+
+    make_product(0)
+    pl.semaphore_wait(barrier, NO - 1 + 2)
+    start_exchange(0)
+    tell(0)
+    for c in range(1, NC):
+        make_product(c)
+
+    small[2].wait()
+    small[3].wait()
     count_low = counts[down]
     for g in range(SL):
         live[g] = (g < count).astype(jnp.int32)
@@ -78,50 +141,16 @@
             here = jnp.clip(at, 0, SL - 1)
             place = jnp.where(own == me_leaf, here, jnp.where(own < me_leaf, low, high))
             table[d * SL + g] = jnp.where(own < 0, SL + 4, place)
-        table[6 * SL + g] = g
-
-    def make_product(c):
-        loads[c].wait()
-
-        def block(g):
-            value = orb_v[c][g].astype(F32) * potential[g].astype(F32)[None]
-            return value.astype(BF16).reshape(RO, PP)
-
-        for g in range(SL):
-            pools[c][g] = block(g)
-        pools[c][SL + 4] = jnp.zeros((RO, PP), BF16)
-        for j in range(2):
-            staged[c, j] = block(jnp.maximum(count - 2 + j, 0))
-
-    def exchange(c):
-        to_up = pltpu.make_async_remote_copy(
-            src_ref=staged.at[c], dst_ref=pools[c].at[SL:SL + 2], send_sem=ex_send.at[c, 0],
-            recv_sem=ex_recv.at[c, 0], device_id=(up, me), device_id_type=MESH)
-        to_down = pltpu.make_async_remote_copy(
-            src_ref=pools[c].at[0:2], dst_ref=pools[c].at[SL + 2:SL + 4], send_sem=ex_send.at[c, 1],
-            recv_sem=ex_recv.at[c, 1], device_id=(down, me), device_id_type=MESH)
-        return to_up, to_down
-
-    exchanges = [exchange(c) for c in range(NC)]
-
-    def start_exchange(c):
-        for copy in exchanges[c]:
-            copy.start()
-
-    make_product(0)
-    pl.semaphore_wait(barrier, G - 1 + NZ - 1 + 2)
-    start_exchange(0)
-    for c in range(1, NC):
-        make_product(c)
-
-    shift = CO.bit_length() - 1
-    rise = (iota((RO, D), 0) >> shift == iota((RO, D), 1)).astype(BF16)
+
     TD = T * D
     lanes = T * RO
-    wide_a, wide_b = iota((TD, lanes), 0), iota((TD, lanes), 1)
-    widen = ((wide_a // D == wide_b // RO) & (lax.rem(wide_a, D) == lax.rem(wide_b, D))).astype(BF16)
-    same = lax.rem(iota((RO, lanes), 0), CO) == lax.rem(iota((RO, lanes), 1), RO) // D
-
+    rise = (split(iota((RO, D), 0), CO)[0] == iota((RO, D), 1)).astype(BF16)
+    term_a, depth_a = split(iota((TD, lanes), 0), D)
+    term_b, rest_b = split(iota((TD, lanes), 1), RO)
+    widen = ((term_a == term_b) & (depth_a == split(rest_b, D)[1])).astype(BF16)
+    same = split(iota((RO, lanes), 0), CO)[1] == split(split(iota((RO, lanes), 1), RO)[1], D)[0]
+
+    small[4].wait()
     for d in range(7):
         tall = lax.dot_general(rise, axis[d], (((1,), (1,)), ((), ())), preferred_element_type=F32).astype(BF16)
         full_d = jnp.dot(tall, widen, preferred_element_type=F32)
@@ -129,28 +158,24 @@
 
     pair_load.wait()
     QB = PP // T
-    row, column = iota((PP, PP), 0), iota((PP, PP), 1)
-    sort = ((row // QB == lax.rem(column, T)) & (lax.rem(row, QB) == column // T)).astype(BF16)
+    sort = reorder(QB, T)
     for d in range(7):
         for q in range(0, PP, QB):
             block = jnp.dot(sort, raw_v[d, q:q + QB].reshape(PP, PP), preferred_element_type=F32).astype(BF16)
             for r in range(T):
                 pair_v[d, r, q:q + QB] = block[r * QB:(r + 1) * QB]
 
-    def pair_step(c, d):
-        for g in range(SL):
-            source[g * RO:(g + 1) * RO, :] = pools[c][table[d * SL + g]]
+    def pair_step(c, d, slots):
+        first = slots[0]
+        many = source.at[first * RO:(slots[-1] + 1) * RO]
+        if d < 6:
+            for g in slots:
+                source[g * RO:(g + 1) * RO, :] = pools[c][table[d * SL + g]]
         for r in range(T):
-            value = jnp.dot(source[...], pair_v[d, r], preferred_element_type=F32).astype(BF16)
-            for g in range(SL):
-                inner[c % 2, g, d, r] = value[g * RO:(g + 1) * RO]
-
-    def self_step(c):
-        for r in range(T):
-            own_blocks = pools[c][0:SL].reshape(SL * RO, PP)
-            value = jnp.dot(own_blocks, pair_v[6, r], preferred_element_type=F32).astype(BF16)
-            for g in range(SL):
-                inner[c % 2, g, 6, r] = value[g * RO:(g + 1) * RO]
+            left = many[...] if d < 6 else pools[c][first:slots[-1] + 1].reshape(len(slots) * RO, PP)
+            value = jnp.dot(left, pair_v[d, r], preferred_element_type=F32).astype(BF16)
+            for i, g in enumerate(slots):
+                inner[c % 2, g, d, r] = value[i * RO:(i + 1) * RO]
 
     rows = ZD * CO
 
@@ -181,31 +206,37 @@
                 rows_v[g * ZD + k, c * NO * CO:(c + 1) * NO * CO, :] = (
                     block[:, k].reshape(NO * CO, PP).astype(BF16))
 
+    every = tuple(range(SL))
     start_exchange(1)
-    self_step(0)
-    self_step(1)
+    for c in range(2):
+        pair_step(c, 6, every)
     for c in range(NC):
         for copy in exchanges[c]:
             copy.wait_recv()
         if c + 2 < NC:
             start_exchange(c + 2)
-        if c >= 2:
-            self_step(c)
-
-        for d in range(6):
-            pair_step(c, d)
-        for g in range(SL):
-            weights = inner[c % 2, g].reshape(7 * T * RO, PP)
-            total = jnp.dot(spread[...], weights, preferred_element_type=F32)
-            total = jnp.where(live[g] > 0, total, 0.0).astype(BF16)
-            for j in range(NO):
-                send1[c, j, g * rows:(g + 1) * rows, :] = total[j * rows:(j + 1) * rows]
-            if c == NC - 1:
-                for t in range(1, NO):
-                    to_peer(c, t, g).start()
+        for slots in (every,) if c < NC - 1 else (every[:3], every[3:]):
+            for d in range(6 if c < 2 else 7):
+                pair_step(c, d, slots)
+            for g in slots:
+                weights = inner[c % 2, g].reshape(7 * T * RO, PP)
+                total = jnp.dot(spread[...], weights, preferred_element_type=F32)
+                total = jnp.where(live[g] > 0, total, 0.0).astype(BF16)
+                for j in range(NO):
+                    send1[c, j, g * rows:(g + 1) * rows, :] = total[j * rows:(j + 1) * rows]
+                if c == NC - 1:
+                    for t in range(1, NO):
+                        to_peer(c, t, g).start()
         if c < NC - 1:
             for t in range(1, NO):
                 to_peer(c, t).start()
+            for i in (2 * c, 2 * c + 1):
+                if i < len(reaches):
+                    hear(i)
+                    if i + 1 < len(reaches):
+                        tell(i + 1)
+                    else:
+                        tell_orbs()
         recv1[me, c] = send1[c, me]
         if c >= 1:
             assemble(c - 1)
@@ -217,6 +248,8 @@
         term = lax.dot_general(block, block, (((1,), (1,)), ((), ())), preferred_element_type=F32)
         total = term if total is None else total + term
     S[...] = total
+
+    pl.semaphore_wait(known.at[len(reaches)], NO - 1)
 
     def p1(q_from, q_to, q_dev):
         return pltpu.make_async_remote_copy(
@@ -328,8 +361,7 @@
     stores = [pltpu.make_async_copy(placed.at[g], out.at[g], out_sem.at[g]) for g in range(SL)]
     for load in loads:
         load.start()
-    row, column = iota((D * 16, D * 16), 0), iota((D * 16, D * 16), 1)
-    swap = ((row // D == lax.rem(column, 16)) & (lax.rem(row, D) == column // 16)).astype(BF16)
+    swap = reorder(D, 16)
     for g in range(SL):
         loads[g].wait()
         for h in range(OL // 16):
@@ -346,17 +378,20 @@
     NC, NZ, G = OL // CO, NL // NX, NX * NO
     ZD, RO, N = D // NO, CO * D, OL * NO
     PR = N // G
-    vmem = pl.BlockSpec(memory_space=pltpu.VMEM)
-    smem = pl.BlockSpec(memory_space=pltpu.SMEM)
     anywhere = pl.BlockSpec(memory_space=pl.ANY)
     dma = pltpu.SemaphoreType.DMA
     blocks = pl.pallas_call(
         functools.partial(kernel, dims),
         out_shape=jax.ShapeDtypeStruct((NO, SL, ZD * OL, PP), BF16),
-        in_specs=[smem, smem, smem, vmem, vmem, anywhere, anywhere],
+        in_specs=[anywhere] * 7,
         out_specs=anywhere,
         scratch_shapes=[
-            pltpu.SMEM((7 * SL,), jnp.int32),
+            pltpu.SMEM((NL,), jnp.int32),
+            pltpu.SMEM((SL, 6), jnp.int32),
+            pltpu.SMEM((SL, 6), jnp.int32),
+            pltpu.VMEM((SL, D, PP), BF16),
+            pltpu.VMEM((7, T * D, D), BF16),
+            pltpu.SMEM((6 * SL,), jnp.int32),
             pltpu.SMEM((SL,), jnp.int32),
             pltpu.VMEM((7, PP, T, PP), BF16),
             pltpu.VMEM((7, T, PP, PP), BF16),
@@ -377,7 +412,7 @@
             dma((NC,)), dma(()), dma((NC, 2)), dma((NC, 2)),
             dma((NC - 1 + SL, NO)), dma((NC - 1 + SL, NO)),
             dma((G,)), dma((G,)), dma((NZ,)), dma((NZ,)), dma((G,)), dma((G,)),
-            dma((SL, NO)), dma((SL, NO)), dma((SL,)),
+            dma((SL, NO)), dma((SL, NO)), dma((SL,)), dma((5,)), pltpu.SemaphoreType.REGULAR((8,)),
         ],
         compiler_params=pltpu.CompilerParams(
             collective_id=0, has_side_effects=True, vmem_limit_bytes=56 * 2**20),

time: 83.9 us -> 82.8 us (0.987)
  Pallas kernels: 83.6 us -> 82.5 us
    pallas_call x1, Pallas kernels: 80.7 us -> 79.6 us  [on_device(): pl.pallas_call(functools.partial(kernel, dims), out_shape=jax.ShapeDtypeS...]
where the time goes in v3:
time: 82.8 us; the launch traced here: 82.7 us
  Pallas kernels  82.5 us (100%)
    pallas_call x1, Pallas kernels, on_device(): pl.pallas_call(functools.partial(kernel, dims), out_shape=jax.ShapeDtypeS...  79.6 us
    pallas_call x1, Pallas kernels, on_device(): pl.pallas_call(functools.partial(settle, dims), out_shape=jax.ShapeDtypeS...  2.92 us

profile of v3, /device:TPU:1, one launch (start us, length us, event | category | flops | bytes accessed | tf_op | source)
XLA Modules:
  0.0 82.7 jit_solution(3135935485715590348)
XLA Ops:
  0.0 79.6 %shard_map.73.blocks = bf16[8,5,64,256]{3,2,1,0:T(8,128)(2,1)} custom-call(s32[32]{0:T(128)} %counts_in.1, s32[5,6]{1,0:T(8,128)} %owner_in.1, s32[5,6]{1,0:T(8,128)} %slot_in.1, bf16[5,16,256]{2,1,0:T(8,128)(2,1)} %potential_in.1, bf16[7,64,16]{2,1,0:T(8,128)(2,1)} %bitcast.1, bf16[5,32,16,256]{3,2,1,0:T(8,128)(2,1)} %orbitals.1, bf16[7,256,4,256]{3,2,1,0:T(4,128)(2,1)} %pair.1), custom_call_target="tpu_custom_call" | custom-call | tf_op jit(solution)/shard_map/pallas_call | solution.py:383
  79.6 2.9 %shard_map.74 = bf16[5,32,16,256]{3,2,1,0:T(8,128)(2,1)} custom-call(bf16[8,5,64,256]{3,2,1,0:T(8,128)(2,1)} %shard_map.73.blocks), custom_call_target="tpu_custom_call" | custom-call | tf_op jit(solution)/shard_map/pallas_call | solution.py:420

commit v4 on v3

--- a/solution.py
+++ b/solution.py
@@ -193,7 +193,7 @@
         peer = lax.rem(me + NO - t, NO)
         return between(c, g, peer, peer, peer)
 
-    def assemble(c):
+    def assemble(c, each=None):
         if c < NC - 1:
             for t in range(1, NO):
                 from_peer(c, t).wait_recv()
@@ -205,6 +205,8 @@
             for k in range(ZD):
                 rows_v[g * ZD + k, c * NO * CO:(c + 1) * NO * CO, :] = (
                     block[:, k].reshape(NO * CO, PP).astype(BF16))
+            if each is not None:
+                each(g)
 
     every = tuple(range(SL))
     start_exchange(1)
@@ -240,14 +242,16 @@
         recv1[me, c] = send1[c, me]
         if c >= 1:
             assemble(c - 1)
-    assemble(NC - 1)
-
-    total = None
-    for k in range(SL * ZD):
-        block = rows_v[k]
-        term = lax.dot_general(block, block, (((1,), (1,)), ((), ())), preferred_element_type=F32)
-        total = term if total is None else total + term
-    S[...] = total
+
+    def intersect(g):
+        total = S[...] if g else None
+        for k in range(g * ZD, (g + 1) * ZD):
+            block = rows_v[k]
+            term = lax.dot_general(block, block, (((1,), (1,)), ((), ())), preferred_element_type=F32)
+            total = term if total is None else total + term
+        S[...] = total
+
+    assemble(NC - 1, intersect)
 
     pl.semaphore_wait(known.at[len(reaches)], NO - 1)
 

time: 82.8 us -> 82.3 us (level)
  no operation moved by 1% of the time
where the time goes in v4:
time: 82.3 us; the launch traced here: 82.2 us
  Pallas kernels  82 us (100%)
    pallas_call x1, Pallas kernels, on_device(): pl.pallas_call(functools.partial(kernel, dims), out_shape=jax.ShapeDtypeS...  79.1 us
    pallas_call x1, Pallas kernels, on_device(): pl.pallas_call(functools.partial(settle, dims), out_shape=jax.ShapeDtypeS...  2.92 us

profile of v4, /device:TPU:1, one launch (start us, length us, event | category | flops | bytes accessed | tf_op | source)
XLA Modules:
  0.0 82.2 jit_solution(263350785274674642)
XLA Ops:
  0.0 79.1 %shard_map.73.blocks = bf16[8,5,64,256]{3,2,1,0:T(8,128)(2,1)} custom-call(s32[32]{0:T(128)} %counts_in.1, s32[5,6]{1,0:T(8,128)} %owner_in.1, s32[5,6]{1,0:T(8,128)} %slot_in.1, bf16[5,16,256]{2,1,0:T(8,128)(2,1)} %potential_in.1, bf16[7,64,16]{2,1,0:T(8,128)(2,1)} %bitcast.1, bf16[5,32,16,256]{3,2,1,0:T(8,128)(2,1)} %orbitals.1, bf16[7,256,4,256]{3,2,1,0:T(4,128)(2,1)} %pair.1), custom_call_target="tpu_custom_call" | custom-call | tf_op jit(solution)/shard_map/pallas_call | solution.py:387
  79.1 2.9 %shard_map.74 = bf16[5,32,16,256]{3,2,1,0:T(8,128)(2,1)} custom-call(bf16[8,5,64,256]{3,2,1,0:T(8,128)(2,1)} %shard_map.73.blocks), custom_call_target="tpu_custom_call" | custom-call | tf_op jit(solution)/shard_map/pallas_call | solution.py:424
